TPU v7x, 32 devices: a whole 2x2x4 slice. The times are simulated.
32 devices in a mesh: dp: 8 (over z, x), tensor: 4 (over y, core).
Axes of the slice: x: 2, y: 2, z: 4, core: 2. Of those that a mesh axis runs over, the one named last changes fastest.
Arguments:
- tokens: bfloat16 [1024, 9216], P(('dp', 'tensor')), may hold values from -6 to 6
- gain: bfloat16 [9216], replicated, may hold values from 0.25 to 1.75
- up_weight: bfloat16 [2304, 9216], P('tensor', 'dp'), may hold values from -0.0625 to 0.0625
- down_weight: bfloat16 [2304, 9216], P('tensor', 'dp'), may hold values from -0.125 to 0.125
- grad_out: bfloat16 [1024, 9216], P(('dp', 'tensor')), may hold values from -6 to 6
Outputs:
- grad_tokens: bfloat16 [1024, 9216], P(('dp', 'tensor'))
- grad_gain: float32 [9216], replicated
- grad_up: bfloat16 [2304, 9216], P('tensor', 'dp')
- grad_down: bfloat16 [2304, 9216], P('tensor', 'dp')
All inputs are finite; a program needn't handle non-finite values.
Results may differ from a plain program's by a relative error of at most 0.012.
Values may be sent and summed in bfloat16 or wider, within the bound.
A program may use at most 128 MiB of HBM per device.

v0:
```python
import jax
import jax.numpy as jnp
from jax import lax
from jax.sharding import PartitionSpec as P

epsilon = 1e-05


def normalize(raw_rows, gain_float):
    floated = raw_rows.astype(jnp.float32)
    inv_rms = lax.rsqrt(jnp.mean(floated * floated, axis=-1, keepdims=True) + epsilon)
    unit_rows = floated * inv_rms
    return (inv_rms, unit_rows, (unit_rows * gain_float).astype(jnp.bfloat16))


def local(tokens, gain, up_weight, down_weight, grad_out):
    gain_float = gain.astype(jnp.float32)
    inv_rms, unit_rows, normed = normalize(tokens, gain_float)
    normed_all, grads_all = (
        lax.all_gather(normed, "tensor", axis=0, tiled=True),
        lax.all_gather(grad_out, "tensor", axis=0, tiled=True),
    )
    up_all, down_all = (
        lax.all_gather(up_weight, "dp", axis=1, tiled=True),
        lax.all_gather(down_weight, "dp", axis=1, tiled=True),
    )
    contract_last = (((1,), (1,)), ((), ()))
    pre_act = lax.dot_general(normed_all, up_all, contract_last, preferred_element_type=jnp.float32)
    back_act = lax.dot_general(
        grads_all, down_all, contract_last, preferred_element_type=jnp.float32
    )
    lifted = jnp.maximum(pre_act, 0.0)
    hidden_act = (lifted * lifted).astype(jnp.bfloat16)
    grad_pre = (back_act * (2.0 * lifted)).astype(jnp.bfloat16)
    contract_rows = (((0,), (0,)), ((), ()))
    term_up = lax.dot_general(
        grad_pre, normed_all, contract_rows, preferred_element_type=jnp.float32
    )
    term_down = lax.dot_general(
        hidden_act, grads_all, contract_rows, preferred_element_type=jnp.float32
    )
    sum_up = lax.psum_scatter(term_up.astype(jnp.bfloat16), "dp", scatter_dimension=1, tiled=True)
    sum_down = lax.psum_scatter(
        term_down.astype(jnp.bfloat16), "dp", scatter_dimension=1, tiled=True
    )
    grad_normed = lax.psum_scatter(
        jnp.dot(grad_pre, up_all, preferred_element_type=jnp.float32).astype(jnp.bfloat16),
        "tensor",
        scatter_dimension=0,
        tiled=True,
    ).astype(jnp.float32)
    gain_terms = jnp.sum(grad_normed * unit_rows, axis=0)
    grad_gain = lax.psum(gain_terms, ("dp", "tensor"))
    grad_unit = grad_normed * gain_float
    mean_term = jnp.mean(grad_unit * unit_rows, axis=-1, keepdims=True)
    grad_tokens = (inv_rms * (grad_unit - unit_rows * mean_term)).astype(jnp.bfloat16)
    return (grad_tokens, grad_gain, sum_up, sum_down)


def solution(mesh):
    placed = (
        P(("dp", "tensor"), None),
        P(),
        P("tensor", "dp"),
        P("tensor", "dp"),
        P(("dp", "tensor"), None),
    )
    return jax.shard_map(
        local,
        mesh=mesh,
        in_specs=placed,
        out_specs=(P(("dp", "tensor"), None), P(), P("tensor", "dp"), P("tensor", "dp")),
        check_vma=False,
    )
```

profile of v0, /device:TPU:0, one launch (start us, length us, event | category | flops | bytes accessed | tf_op | source)
XLA Modules:
  0.0 824.7 jit_solution(15398528423835322744)
XLA Ops:
  7.2 0.7 convert_element_type.31
  7.9 1.3 fusion.8
  9.2 2.1 fusion.6
  11.3 0.0 all-gather.11.cloned.1.call-start
  11.4 0.7 all-gather.11.cloned.1.call-update
  12.1 0.0 all-gather.5.cloned.1.call-start
  12.1 0.7 all-gather.5.cloned.1.call-update
  12.9 0.5 all-gather.7.cloned.1.call-update
  13.4 0.0 reduce-scatter.8.cloned.1.call-start
  13.5 24.8 %all-gather.9.cloned.1.call-done = bf16[128,9216]{1,0:T(8,128)(2,1)} async-done(((bf16[32,9216]{1,0:T(8,128)(2,1)}), bf16[128,9216]{1,0:T(8,128)(2,1)}) %all-gather.9.cloned.1.call-update) | async-done | bytes 2359312 | tf_op jit(solution)/shard_map/all_gather | solution.py:20
  38.3 154.8 %all-gather.11.cloned.1.call-done = bf16[576,9216]{1,0:T(8,128)(2,1)} async-done(((bf16[576,1152]{1,0:T(8,128)(2,1)}), bf16[576,9216]{1,0:T(8,128)(2,1)}) %all-gather.11.cloned.1.call-update) | async-done | bytes 10616848 | tf_op jit(solution)/shard_map/all_gather | solution.py:24
  193.1 6.4 convolution_maximum_fusion
  199.4 17.5 %all-gather.5.cloned.1.call-done = bf16[128,9216]{1,0:T(8,128)(2,1)} async-done(((bf16[32,9216]{1,0:T(8,128)(2,1)}), bf16[128,9216]{1,0:T(8,128)(2,1)}) %all-gather.5.cloned.1.call-update) | async-done | bytes 2359312 | tf_op jit(solution)/shard_map/all_gather | solution.py:21
  216.9 154.7 %all-gather.7.cloned.1.call-done = bf16[576,9216]{1,0:T(8,128)(2,1)} async-done(((bf16[576,1152]{1,0:T(8,128)(2,1)}), bf16[576,9216]{1,0:T(8,128)(2,1)}) %all-gather.7.cloned.1.call-update) | async-done | bytes 10616848 | tf_op jit(solution)/shard_map/all_gather | solution.py:25
  371.6 7.8 fusion.10
  379.4 3.6 convolution_convert_fusion.2
  383.0 0.0 reduce-scatter.10.cloned.1.call-start
  383.0 1.6 copy-done.1
  384.6 5.7 convolution_convert_fusion.1
  390.3 15.7 %copy.9 = bf16[576,9216]{0,1:T(8,128)(2,1)} copy(bf16[576,9216]{1,0:T(8,128)(2,1)} %convolution_convert_fusion.1) | data formatting | bytes 21233664
  406.1 0.0 reduce-scatter.12.cloned.1.call-start
  406.1 1.6 copy-done.2
  407.7 5.5 convolution_convert_fusion
  413.3 15.7 %copy.11 = bf16[576,9216]{0,1:T(8,128)(2,1)} copy(bf16[576,9216]{1,0:T(8,128)(2,1)} %convolution_convert_fusion) | data formatting | bytes 21233664
  429.1 1.0 copy-done.3
  430.1 1.6 fusion.9
  431.7 42.6 %psum.7 = f32[9216]{0:T(1024)} all-reduce(f32[9216]{0:T(1024)S(1)} %get-tuple-element.4), channel_id=1, replica_groups=mesh['dp'=8,'tensor'=4] {'dp','tensor'}, use_global_device_ids=true, to_apply=%region_4.0 | all-reduce | flops 9216 | bytes 73728 | tf_op jit(solution)/shard_map/psum | solution.py:53
  474.3 2.3 fusion.5
  476.5 139.6 %reduce-scatter.10.cloned.1.call-done = bf16[1152,576]{1,0:T(8,128)(2,1)} async-done(((bf16[9216,576]{1,0:T(8,128)(2,1)}), bf16[1152,576]{1,0:T(8,128)(2,1)}) %reduce-scatter.10.cloned.1.call-update) | async-done | bytes 1327120
  616.2 2.6 copy.10
  618.7 196.5 %reduce-scatter.12.cloned.1.call-done = bf16[1152,576]{1,0:T(8,128)(2,1)} async-done(((bf16[9216,576]{1,0:T(8,128)(2,1)}), bf16[1152,576]{1,0:T(8,128)(2,1)}) %reduce-scatter.12.cloned.1.call-update) | async-done | bytes 1327120
  815.3 2.6 copy.12
  (14 shorter events, 0.2 us)
Async XLA Ops:
  7.2 31.1 %all-gather.9.cloned.1.call-start = ((), (), s32[]{:S(2)}) async-start(), calls=%async_computation.5 | async-start | bytes 2949120 | tf_op jit(solution)/shard_map/all_gather | solution.py:20
  11.3 181.7 %all-gather.11.cloned.1.call-start = ((), (), s32[]{:S(2)}) async-start(), calls=%async_computation.6 | async-start | bytes 11943936 | tf_op jit(solution)/shard_map/all_gather | solution.py:24
  12.1 204.8 %all-gather.5.cloned.1.call-start = ((), (), s32[]{:S(2)}) async-start(), calls=%async_computation.3 | async-start | bytes 2949120 | tf_op jit(solution)/shard_map/all_gather | solution.py:21
  12.8 358.7 %all-gather.7.cloned.1.call-start = ((), (), s32[]{:S(2)}) async-start(), calls=%async_computation.4 | async-start | bytes 11943936 | tf_op jit(solution)/shard_map/all_gather | solution.py:25
  13.4 415.6 %reduce-scatter.8.cloned.1.call-start = ((), (), s32[]{:S(2)}) async-start(), calls=%async_computation.7 | async-start | bytes 2949120 | tf_op jit(solution)/shard_map/reduce_scatter | solution.py:46
  371.6 7.8 copy-start
  382.9 1.7 copy-start.1
  383.0 233.2 %reduce-scatter.10.cloned.1.call-start = ((), (), s32[]{:S(2)}) async-start(), calls=%async_computation.8 | async-start | bytes 13271040
  406.0 1.7 copy-start.2
  406.1 409.2 %reduce-scatter.12.cloned.1.call-start = ((), (), s32[]{:S(2)}) async-start(), calls=%async_computation.9 | async-start | bytes 13271040
  429.0 1.1 copy-start.3
Sparse Core Ops, SparseCore 0:
  11.5 26.7 all-gather.8
  40.6 152.4 all-gather.10
  194.6 22.2 all-gather.4
  219.1 152.4 all-gather.6
  383.1 31.2 reduce-scatter.7
  418.3 197.8 reduce-scatter.9
  619.8 195.4 reduce-scatter.11
where the time goes:
time: 826 us; the launch traced here: 825 us
  waiting for transfers between devices  690 us (84%)
  blocking collectives  42.6 us (5%)
  local copies, waits for them, and re-layouts  40.8 us (5%)
  matrix products  29 us (4%)
  between operations  14.2 us (2%)
    unnamed x9, waiting for transfers between devices  338 us
    all_gather x1, waiting for transfers between devices, local(): lax.all_gather(up_weight, 'dp', axis=1, tiled=True)  155 us
    all_gather x1, waiting for transfers between devices, local(): lax.all_gather(down_weight, 'dp', axis=1, tiled=True)  155 us
    psum x1, blocking collectives, local(): grad_gain = lax.psum(gain_terms, ('dp', 'tensor'))  42.6 us
    unnamed x12, local copies, waits for them, and re-layouts  40.8 us
    all_gather x1, waiting for transfers between devices, local(): lax.all_gather(normed, 'tensor', axis=0, tiled=True)  24.8 us
    all_gather x1, waiting for transfers between devices, local(): lax.all_gather(grad_out, 'tensor', axis=0, tiled=True)  17.5 us
  transfers between devices with their start and end apart: 7, of which 6 were waited for; matrix products, arithmetic and copies ran while one was open for 7% of the time, Pallas kernels for 0%

commit v1 on v0

v1 whole, which is shorter than its diff:
```python
import jax
import jax.numpy as jnp
from jax import lax
from jax.sharding import PartitionSpec as P

epsilon = 1e-05


def local(tokens, gain, up_weight, down_weight, grad_out):
    gain_float = gain.astype(jnp.float32)
    floated = tokens.astype(jnp.float32)
    inv_rms = lax.rsqrt(jnp.mean(floated * floated, axis=-1, keepdims=True) + epsilon)
    unit_rows = floated * inv_rms
    normed = (unit_rows * gain_float).astype(jnp.bfloat16)

    def to_columns(rows):
        part = lax.all_to_all(rows, "dp", split_axis=1, concat_axis=0, tiled=True)
        return lax.all_gather(part, "tensor", axis=0, tiled=True)

    grads_cols = to_columns(grad_out)
    normed_cols = to_columns(normed)
    contract_last = (((1,), (1,)), ((), ()))
    back_part = lax.dot_general(
        grads_cols, down_weight, contract_last, preferred_element_type=jnp.float32
    ).astype(jnp.bfloat16)
    pre_part = lax.dot_general(
        normed_cols, up_weight, contract_last, preferred_element_type=jnp.float32
    ).astype(jnp.bfloat16)
    back_act = lax.psum_scatter(back_part, "dp", scatter_dimension=0, tiled=True)
    pre_act = lax.psum_scatter(pre_part, "dp", scatter_dimension=0, tiled=True)
    lifted = jnp.maximum(pre_act.astype(jnp.float32), 0.0)
    hidden_part = (lifted * lifted).astype(jnp.bfloat16)
    grad_pre_part = (back_act.astype(jnp.float32) * (2.0 * lifted)).astype(jnp.bfloat16)
    grad_pre = lax.all_gather(grad_pre_part, "dp", axis=0, tiled=True)
    hidden_act = lax.all_gather(hidden_part, "dp", axis=0, tiled=True)
    grad_normed_part = jnp.dot(
        grad_pre, up_weight, preferred_element_type=jnp.float32
    ).astype(jnp.bfloat16)
    grad_normed = lax.psum_scatter(grad_normed_part, "tensor", scatter_dimension=0, tiled=True)
    grad_normed = lax.all_to_all(
        grad_normed, "dp", split_axis=0, concat_axis=1, tiled=True
    ).astype(jnp.float32)
    contract_rows = (((0,), (0,)), ((), ()))
    grad_up = lax.dot_general(
        grad_pre, normed_cols, contract_rows, preferred_element_type=jnp.float32
    ).astype(jnp.bfloat16)
    grad_down = lax.dot_general(
        hidden_act, grads_cols, contract_rows, preferred_element_type=jnp.float32
    ).astype(jnp.bfloat16)
    grad_gain = lax.psum(jnp.sum(grad_normed * unit_rows, axis=0), ("dp", "tensor"))
    grad_unit = grad_normed * gain_float
    mean_term = jnp.mean(grad_unit * unit_rows, axis=-1, keepdims=True)
    grad_tokens = (inv_rms * (grad_unit - unit_rows * mean_term)).astype(jnp.bfloat16)
    return (grad_tokens, grad_gain, grad_up, grad_down)


def solution(mesh):
    rows = P(("dp", "tensor"), None)
    weights = P("tensor", "dp")
    return jax.shard_map(
        local,
        mesh=mesh,
        in_specs=(rows, P(), weights, weights, rows),
        out_specs=(rows, P(), weights, weights),
        check_vma=False,
    )
```

time: 826 us -> 398 us (0.48)
  waiting for transfers between devices: 690 us -> 264 us
  blocking collectives: 42.6 us -> 82.7 us
  local copies, waits for them, and re-layouts: 40.8 us -> 6.32 us
    all_gather x4, waiting for transfers between devices: 352 us -> 102 us  [the longest x1 40.5 us: local(): grad_pre = lax.all_gather(grad_pre_part, 'dp', axis=0, tiled=True)]
    unnamed x9, waiting for transfers between devices: 338 us -> 130 us
    all_to_all x0 -> x2, blocking collectives: none -> 43.1 us  [to_columns(): part = lax.all_to_all(rows, 'dp', split_axis=1, concat_axis=0, tiled=True)]
    unnamed x12 -> x10, local copies, waits for them, and re-layouts: 40.8 us -> 4.99 us
    reduce_scatter x1, waiting for transfers between devices: 0.02 us -> 31.3 us  [local(): lax.psum_scatter(grad_normed_part, 'tensor', scatter_dimension=0, tiled=T...]
  transfers between devices with their start and end apart: 7 -> 8, of which waited for: 6 -> 7; matrix products, arithmetic and copies ran while one was open for 7% -> 5% of each run, Pallas kernels for 0% -> 0%
where the time goes in v1:
time: 398 us; the launch traced here: 397 us
  waiting for transfers between devices  264 us (66%)
  blocking collectives  82.7 us (21%)
  matrix products  21.6 us (5%)
  between operations  14.2 us (4%)
  local copies, waits for them, and re-layouts  6.32 us (2%)
  starting transfers between devices  5.78 us (1%)
    unnamed x9, waiting for transfers between devices  130 us
    all_to_all x2, blocking collectives, to_columns(): part = lax.all_to_all(rows, 'dp', split_axis=1, concat_axis=0, tiled=True)  43.1 us
    all_gather x1, waiting for transfers between devices, local(): grad_pre = lax.all_gather(grad_pre_part, 'dp', axis=0, tiled=True)  40.5 us
    psum x1, blocking collectives, local(): lax.psum(jnp.sum(grad_normed * unit_rows, axis=0), ('dp', 'tensor'))  39.6 us
    all_gather x1, waiting for transfers between devices, local(): hidden_act = lax.all_gather(hidden_part, 'dp', axis=0, tiled=True)  38.3 us
    reduce_scatter x1, waiting for transfers between devices, local(): lax.psum_scatter(grad_normed_part, 'tensor', scatter_dimension=0, tiled=T...  31.3 us
    all_gather x2, waiting for transfers between devices, to_columns(): return lax.all_gather(part, 'tensor', axis=0, tiled=True)  23.1 us
  transfers between devices with their start and end apart: 8, of which 7 were waited for; matrix products, arithmetic and copies ran while one was open for 5% of the time, Pallas kernels for 0%

profile of v1, /device:TPU:0, one launch (start us, length us, event | category | flops | bytes accessed | tf_op | source)
XLA Modules:
  0.0 397.5 jit_solution(18426627783304222205)
XLA Ops:
  7.2 1.2 copy.27
  8.5 23.9 %all_to_all.51 = bf16[32,8,1152]{2,0,1:T(8,128)(2,1)} all-to-all(bf16[32,8,1152]{2,0,1:T(8,128)(2,1)S(1)} %bitcast.36), channel_id=1, replica_groups=mesh['dp'=8,'tensor'=4] {'dp'}, dimensions={1} | all-to-all | bytes 1179648 | tf_op jit(solution)/shard_map/all_to_all | solution.py:17
  32.3 0.0 all-gather.7.cloned.1.call-start
  32.4 0.2 fusion.10
  32.7 0.2 fusion.4
  33.0 19.3 %all_to_all.52 = bf16[32,8,1152]{2,0,1:T(8,128)(2,1)} all-to-all(bf16[32,8,1152]{2,0,1:T(8,128)(2,1)S(1)} %bitcast.35), channel_id=1, replica_groups=mesh['dp'=8,'tensor'=4] {'dp'}, dimensions={1} | all-to-all | bytes 1179648 | tf_op jit(solution)/shard_map/all_to_all | solution.py:17
  52.2 0.0 reduce-scatter.10.cloned.1.call-start
  52.3 2.7 all-gather.5.cloned.1.call-done
  55.0 3.7 convolution_convert_fusion.4
  58.7 1.4 copy.17
  60.2 0.0 reduce-scatter.12.cloned.1.call-start
  60.2 20.4 %all-gather.7.cloned.1.call-done = bf16[1024,1152]{1,0:T(8,128)(2,1)} async-done(((bf16[256,1152]{1,0:T(8,128)(2,1)}), bf16[1024,1152]{1,0:T(8,128)(2,1)}) %all-gather.7.cloned.1.call-update) | async-done | bytes 2359312 | tf_op jit(solution)/shard_map/all_gather | solution.py:18
  80.6 3.4 convolution_convert_fusion.3
  84.0 1.4 copy.19
  85.5 63.4 %reduce-scatter.10.cloned.1.call-done = bf16[128,576]{1,0:T(8,128)(2,1)} async-done(((bf16[1024,576]{1,0:T(8,128)(2,1)}), bf16[128,576]{1,0:T(8,128)(2,1)}) %reduce-scatter.10.cloned.1.call-update) | async-done | bytes 147472
  149.0 1.1 copy.18
  150.0 66.2 %reduce-scatter.12.cloned.1.call-done = bf16[128,576]{1,0:T(8,128)(2,1)} async-done(((bf16[1024,576]{1,0:T(8,128)(2,1)}), bf16[128,576]{1,0:T(8,128)(2,1)}) %reduce-scatter.12.cloned.1.call-update) | async-done | bytes 147472
  216.3 1.1 copy.20
  217.3 0.8 multiply_convert_fusion
  218.2 40.5 %all-gather.9.cloned.1.call-done = bf16[1024,576]{0,1:T(8,128)(2,1)} async-done(((bf16[128,576]{0,1:T(8,128)(2,1)}), bf16[1024,576]{0,1:T(8,128)(2,1)}) %all-gather.9.cloned.1.call-update) | async-done | bytes 1179664 | tf_op jit(solution)/shard_map/all_gather | solution.py:34
  258.7 4.9 %convolution_convert_fusion = bf16[1024,1152]{1,0:T(8,128)(2,1)} fusion(bf16[1024,576]{0,1:T(8,128)(2,1)} %all-gather.9.cloned.1.call-done, bf16[576,1152]{1,0:T(8,128)(2,1)S(1)} %copy-done), kind=kOutput, calls=%fused_computation | convolution fusion | flops 1360134144 | bytes 4866048 | tf_op jit(solution)/shard_map/dot_general | solution.py:36
  263.7 0.7 all-gather.11.cloned.1.call-update
  264.4 31.3 %reduce-scatter.8.cloned.1.call-done = bf16[256,1152]{1,0:T(8,128)(2,1)} async-done(((bf16[1024,1152]{1,0:T(8,128)(2,1)}), bf16[256,1152]{1,0:T(8,128)(2,1)}) %reduce-scatter.8.cloned.1.call-update) | async-done | bytes 589840 | tf_op jit(solution)/shard_map/reduce_scatter | solution.py:39
  295.7 5.5 %all-to-all-start.2 = ((bf16[8,32,1152]{2,1,0:T(8,128)(2,1)}), bf16[8,32,1152]{2,1,0:T(8,128)(2,1)S(1)}, u32[]{:S(2)}, u32[]{:S(2)}) async-start(bf16[8,32,1152]{2,1,0:T(8,128)(2,1)} %bitcast.39), calls=%async_computation.3 | async-start | bytes 1179648 | tf_op jit(solution)/shard_map/all_to_all | solution.py:40
  301.2 4.8 %convolution_convert_fusion.2 = bf16[576,1152]{1,0:T(8,128)(2,1)} fusion(bf16[1024,576]{0,1:T(8,128)(2,1)} %all-gather.9.cloned.1.call-done, bf16[1024,1152]{1,0:T(8,128)(2,1)} %all-gather.7.cloned.1.call-done), kind=kOutput, calls=%fused_computation.2 | convolution fusion | flops 1359618048 | bytes 4866048 | tf_op jit(solution)/shard_map/dot_general | solution.py:44
  306.0 38.3 %all-gather.11.cloned.1.call-done = bf16[1024,576]{0,1:T(8,128)(2,1)} async-done(((bf16[128,576]{0,1:T(8,128)(2,1)}), bf16[1024,576]{0,1:T(8,128)(2,1)}) %all-gather.11.cloned.1.call-update) | async-done | bytes 1179664 | tf_op jit(solution)/shard_map/all_gather | solution.py:35
  344.3 4.8 %convolution_convert_fusion.1 = bf16[576,1152]{1,0:T(8,128)(2,1)} fusion(bf16[1024,576]{0,1:T(8,128)(2,1)} %all-gather.11.cloned.1.call-done, bf16[1024,1152]{1,0:T(8,128)(2,1)} %all-gather.5.cloned.1.call-done), kind=kOutput, calls=%fused_computation.1 | convolution fusion | flops 1359618048 | bytes 4866048 | tf_op jit(solution)/shard_map/dot_general | solution.py:47
  349.1 0.1 convert_bitcast_fusion
  349.2 0.1 copy.23
  349.3 0.6 fusion.9
  349.9 39.6 %psum.7 = f32[9216]{0:T(1024)} all-reduce(f32[9216]{0:T(1024)S(1)} %get-tuple-element.4), channel_id=1, replica_groups=mesh['dp'=8,'tensor'=4] {'dp','tensor'}, use_global_device_ids=true, to_apply=%region_6.0 | all-reduce | flops 9216 | bytes 73728 | tf_op jit(solution)/shard_map/psum | solution.py:50
  389.5 1.1 fusion.8
  (21 shorter events, 0.3 us)
Async XLA Ops:
  7.2 73.5 %copy-start = (bf16[576,1152]{1,0:T(8,128)(2,1)S(1)}, bf16[576,1152]{1,0:T(8,128)(2,1)}, u32[]{:S(2)}) copy-start(bf16[576,1152]{1,0:T(8,128)(2,1)} %param.7) | copy-start | bytes 3981316
  7.2 47.8 %all-gather.5.cloned.1.call-start = ((), (), s32[]{:S(2)}) async-start(), calls=%async_computation.6 | async-start | bytes 2949120 | tf_op jit(solution)/shard_map/all_gather | solution.py:18
  8.4 24.0 %copy-start.2 = (bf16[9216]{0:T(1024)(128)(2,1)S(1)}, bf16[9216]{0:T(1024)(128)(2,1)}, u32[]{:S(2)}) copy-start(bf16[9216]{0:T(1024)(128)(2,1)} %param.6) | copy-start | bytes 55300
  8.4 24.0 %copy-start.1 = (bf16[32,9216]{1,0:T(8,128)(2,1)S(1)}, bf16[32,9216]{1,0:T(8,128)(2,1)}, u32[]{:S(2)}) copy-start(bf16[32,9216]{1,0:T(8,128)(2,1)} %param.5) | copy-start | bytes 1769476
  32.3 48.3 %all-gather.7.cloned.1.call-start = ((), (), s32[]{:S(2)}) async-start(), calls=%async_computation.7 | async-start | bytes 2949120 | tf_op jit(solution)/shard_map/all_gather | solution.py:18
  52.2 96.8 %reduce-scatter.10.cloned.1.call-start = ((), (), s32[]{:S(2)}) async-start(), calls=%async_computation.11 | async-start | bytes 1474560
  60.2 156.1 %reduce-scatter.12.cloned.1.call-start = ((), (), s32[]{:S(2)}) async-start(), calls=%async_computation.12 | async-start | bytes 1474560
  85.5 173.2 %all-gather.9.cloned.1.call-start = ((), (), s32[]{:S(2)}) async-start(), calls=%async_computation.8 | async-start | bytes 1327104 | tf_op jit(solution)/shard_map/all_gather | solution.py:34
  218.2 77.6 %reduce-scatter.8.cloned.1.call-start = ((), (), s32[]{:S(2)}) async-start(), calls=%async_computation.9 | async-start | bytes 2949120 | tf_op jit(solution)/shard_map/reduce_scatter | solution.py:39
  263.6 80.7 %all-gather.11.cloned.1.call-start = ((), (), s32[]{:S(2)}) async-start(), calls=%async_computation.10 | async-start | bytes 1327104 | tf_op jit(solution)/shard_map/all_gather | solution.py:35
  295.7 53.4 %all-to-all-start.2 = ((bf16[8,32,1152]{2,1,0:T(8,128)(2,1)}), bf16[8,32,1152]{2,1,0:T(8,128)(2,1)S(1)}, u32[]{:S(2)}, u32[]{:S(2)}) async-start(bf16[8,32,1152]{2,1,0:T(8,128)(2,1)} %bitcast.39), calls=%async_computation.3 | async-start | bytes 1179648 | tf_op jit(solution)/shard_map/all_to_all | solution.py:40
Sparse Core Ops, SparseCore 0:
  32.5 22.4 all-gather.4
  56.5 24.0 all-gather.6
  84.6 64.3 reduce-scatter.9
  152.8 63.4 reduce-scatter.11
  218.8 39.9 all-gather.8
  263.8 31.9 reduce-scatter.7
  298.5 45.7 all-gather.10

commit v2 on v1

--- a/solution.py
+++ b/solution.py
@@ -1,7 +1,13 @@
+import functools
+
 import jax
 import jax.numpy as jnp
 from jax import lax
+from jax.experimental import pallas as pl
+from jax.experimental.pallas import tpu as pltpu
 from jax.sharding import PartitionSpec as P
+
+MESH = pl.DeviceIdType.MESH
 
 epsilon = 1e-05
 
@@ -54,11 +60,332 @@
     return (grad_tokens, grad_gain, grad_up, grad_down)
 
 
+def kernel(
+    tokens, gain_row, gain_own, up, down, grad_out,
+    out_tokens, out_gain, out_up, out_down,
+    inv_rms, normed, ncols, gcols, part, recvx, sumz, recvz, gp, hid,
+    esend, ecore, ysend, ey, gnf, gnb, gnrows, gsum, grecv, gshare,
+    a2a_s, a2a_r, tens_s, tens_r, x_s, x_r, z_s, z_r, gz_s, gz_r, gx_s, gx_r,
+    e_s, e_r, back_s, back_r, gt_s, gt_r, gd_s, gd_r,
+):
+    n_dp, n_t, n_z = 8, 4, 4
+    rows, columns = tokens.shape[0], up.shape[1]
+    hidden = up.shape[0]
+    block = n_dp * rows
+    chunk = n_t * rows
+    d, t = lax.axis_index("dp"), lax.axis_index("tensor")
+    z, x = d // 2, d % 2
+    y, c = t // 2, t % 2
+    x_peer = (z * 2 + 1 - x, t)
+    y_peer = (d, (1 - y) * 2 + c)
+    core_peer = (d, y * 2 + 1 - c)
+
+    def dp_peer(k):
+        return (lax.rem(d + k, n_dp), t)
+
+    def z_peer(k):
+        return (lax.rem(z + k, n_z) * 2 + x, t)
+
+    def t_peer(k):
+        return (d, lax.rem(t + k, n_t))
+
+    def send(src, dst, s, r, to):
+        copy = pltpu.make_async_remote_copy(
+            src_ref=src, dst_ref=dst, send_sem=s, recv_sem=r, device_id=to, device_id_type=MESH
+        )
+        copy.start()
+        sent.append(copy)
+
+    sent = []
+
+    def arrived(dst, s, r):
+        pltpu.make_async_remote_copy(
+            src_ref=dst, dst_ref=dst, send_sem=s, recv_sem=r, device_id=x_peer, device_id_type=MESH
+        ).wait_recv()
+
+    def cols_of(i):
+        return pl.ds(pl.multiple_of(i * columns, 128), columns)
+
+    def rows_of(i, size):
+        return pl.ds(pl.multiple_of(i * size, 32), size)
+
+    def lanes_of(i):
+        return pl.ds(pl.multiple_of(i * chunk, 128), chunk)
+
+    barrier = pltpu.get_barrier_semaphore()
+    for k in range(1, n_dp):
+        pl.semaphore_signal(barrier, inc=1, device_id=dp_peer(k), device_id_type=MESH)
+    for k in range(1, n_t):
+        pl.semaphore_signal(barrier, inc=1, device_id=t_peer(k), device_id_type=MESH)
+    pl.semaphore_wait(barrier, n_dp - 1 + n_t - 1)
+
+    own_rows = rows_of(t * n_dp + d, rows)
+    order = (4, 3, 5, 2, 6, 1, 7)
+    for k in order:
+        send(grad_out.at[:, cols_of(lax.rem(d + k, n_dp))], gcols.at[own_rows],
+             a2a_s.at[0, k], a2a_r.at[0, k], dp_peer(k))
+    gcols[own_rows, :] = grad_out[:, cols_of(d)]
+    floated = tokens[...].astype(jnp.float32)
+    inv_rms[...] = lax.rsqrt(jnp.mean(floated * floated, axis=-1, keepdims=True) + epsilon)
+    for i in range(n_dp):
+        s = pl.ds(i * columns, columns)
+        normed[:, s] = (
+            tokens[:, s].astype(jnp.float32) * inv_rms[...] * gain_row[:, s].astype(jnp.float32)
+        ).astype(jnp.bfloat16)
+    for k in order:
+        send(normed.at[:, cols_of(lax.rem(d + k, n_dp))], ncols.at[own_rows],
+             a2a_s.at[1, k], a2a_r.at[1, k], dp_peer(k))
+    ncols[own_rows, :] = normed[:, cols_of(d)]
+
+    own_block = rows_of(t, block)
+    y_block = rows_of((1 - y) * 2 + c, block)
+    core_block = rows_of(y * 2 + 1 - c, block)
+    far_block = rows_of((1 - y) * 2 + 1 - c, block)
+
+    def spread(a, buf):
+        for k in order:
+            arrived(buf.at[rows_of(t * n_dp + lax.rem(d - k + n_dp, n_dp), rows)],
+                    a2a_s.at[a, k], a2a_r.at[a, k])
+        send(buf.at[own_block], buf.at[own_block], tens_s.at[a, 0], tens_r.at[a, 0], y_peer)
+        send(buf.at[own_block], buf.at[own_block], tens_s.at[a, 1], tens_r.at[a, 1], core_peer)
+
+    def spread_far(a, buf):
+        arrived(buf.at[y_block], tens_s.at[a, 0], tens_r.at[a, 0])
+        send(buf.at[y_block], buf.at[y_block], tens_s.at[a, 2], tens_r.at[a, 2], core_peer)
+
+    def spread_wait(a, buf):
+        arrived(buf.at[core_block], tens_s.at[a, 1], tens_r.at[a, 1])
+        arrived(buf.at[far_block], tens_s.at[a, 2], tens_r.at[a, 2])
+
+    def product(a, buf, weight, i):
+        prod = lax.dot_general(
+            weight[...], buf[rows_of(i, block), :], (((1,), (1,)), ((), ())),
+            preferred_element_type=jnp.float32,
+        ).astype(jnp.bfloat16)
+        part[a, i, 0] = prod[:, :chunk]
+        part[a, i, 1] = prod[:, chunk:]
+
+    def to_x(a, i):
+        send(part.at[a, i, 1 - x], recvx.at[a, i], x_s.at[a, i], x_r.at[a, i], x_peer)
+
+    def products(a, buf, weight):
+        for i in range(n_z):
+            product(a, buf, weight, i)
+            to_x(a, i)
+
+    def x_sum(a, i):
+        return part[a, i, x].astype(jnp.float32) + recvx[a, i].astype(jnp.float32)
+
+    def to_z(a):
+        for k in (2, 3, 1):
+            i = lax.rem(z + k, n_z)
+            arrived(recvx.at[a, i], x_s.at[a, i], x_r.at[a, i])
+            sumz[a, k - 1] = x_sum(a, i).astype(jnp.bfloat16)
+            send(sumz.at[a, k - 1], recvz.at[a, k - 1], z_s.at[a, k - 1], z_r.at[a, k - 1],
+                 z_peer(k))
+
+    def z_wait(a):
+        arrived(recvx.at[a, z], x_s.at[a, z], x_r.at[a, z])
+        for k in (1, 2, 3):
+            arrived(recvz.at[a, k - 1], z_s.at[a, k - 1], z_r.at[a, k - 1])
+
+    def z_sum(a, s):
+        total = part[a, z, x, s, :].astype(jnp.float32) + recvx[a, z, s, :].astype(jnp.float32)
+        for k in range(3):
+            total = total + recvz[a, k, s, :].astype(jnp.float32)
+        return total
+
+    spread(0, gcols)
+    spread_far(0, gcols)
+    spread_wait(0, gcols)
+    products(0, gcols, down)
+    spread(1, ncols)
+    to_z(0)
+    spread_far(1, ncols)
+    spread_wait(1, ncols)
+    products(1, ncols, up)
+    to_z(1)
+    z_wait(0)
+    z_wait(1)
+
+    own_lanes = lanes_of(d)
+    whole = pl.ds(0, hidden)
+    lifted = jnp.maximum(z_sum(1, whole), 0.0)
+    gp[:, own_lanes] = (z_sum(0, whole) * (2.0 * lifted)).astype(jnp.bfloat16)
+    hid[:, own_lanes] = (lifted * lifted).astype(jnp.bfloat16)
+
+    def share(a, buf):
+        for k in (2, 1, 3):
+            send(buf.at[:, own_lanes], buf.at[:, own_lanes], gz_s.at[a, k], gz_r.at[a, k],
+                 z_peer(k))
+        send(buf.at[:, own_lanes], buf.at[:, own_lanes], gx_s.at[a, 0], gx_r.at[a, 0], x_peer)
+
+    def z_lanes(k, side):
+        return lanes_of(lax.rem(z - k + n_z, n_z) * 2 + side)
+
+    def share_far(a, buf):
+        for k in (1, 3, 2):
+            s = z_lanes(k, x)
+            arrived(buf.at[:, s], gz_s.at[a, k], gz_r.at[a, k])
+            send(buf.at[:, s], buf.at[:, s], gx_s.at[a, k], gx_r.at[a, k], x_peer)
+
+    def share_wait(a, buf):
+        for k in range(n_z):
+            arrived(buf.at[:, z_lanes(k, 1 - x)], gx_s.at[a, k], gx_r.at[a, k])
+
+    share(0, gp)
+    share(1, hid)
+    share_far(0, gp)
+    share_wait(0, gp)
+
+    def input_part(i):
+        return lax.dot_general(
+            gp[:, pl.ds(pl.multiple_of(i * block, 128), block)], up[...],
+            (((0,), (0,)), ((), ())), preferred_element_type=jnp.float32,
+        )
+
+    for h in range(2):
+        q = 1 - y if h == 0 else y
+        esend[h] = input_part(q * 2 + 1 - c).astype(jnp.bfloat16)
+        send(esend.at[h], ecore.at[h], e_s.at[h], e_r.at[h], core_peer)
+    gnf[...] = input_part((1 - y) * 2 + c)
+    arrived(ecore.at[0], e_s.at[0], e_r.at[0])
+    ysend[...] = (gnf[...] + ecore[0].astype(jnp.float32)).astype(jnp.bfloat16)
+    send(ysend, ey, e_s.at[2], e_r.at[2], y_peer)
+    gnf[...] = input_part(t)
+    arrived(ecore.at[1], e_s.at[1], e_r.at[1])
+    gnf[...] = gnf[...] + ecore[1].astype(jnp.float32)
+    share_far(1, hid)
+    arrived(ey, e_s.at[2], e_r.at[2])
+    gnf[...] = gnf[...] + ey[...].astype(jnp.float32)
+    gnb[...] = gnf[...].astype(jnp.bfloat16)
+    for k in order:
+        send(gnb.at[rows_of(lax.rem(d + k, n_dp), rows)], gnrows.at[:, cols_of(d)],
+             back_s.at[k], back_r.at[k], dp_peer(k))
+    gnrows[:, cols_of(d)] = gnb[rows_of(d, rows), :]
+
+    total = jnp.zeros((8, columns), jnp.float32)
+    for i in range(block // 32):
+        term = gnf[pl.ds(i * 32, 32), :] * ncols[
+            pl.ds(pl.multiple_of(t * block + i * 32, 32), 32), :
+        ].astype(jnp.float32)
+        total = total + term[0:8] + term[8:16] + term[16:24] + term[24:32]
+    gsum[...] = total
+    for k in range(1, n_t):
+        send(gsum, grecv.at[k - 1], gt_s.at[k - 1], gt_r.at[k - 1], t_peer(k))
+
+    def rows_product(left, right, out):
+        half = columns // 3
+        for i in range(3):
+            s = pl.ds(i * half, half)
+            out[:, s] = jnp.dot(
+                left[...], right[:, s], preferred_element_type=jnp.float32
+            ).astype(jnp.bfloat16)
+
+    rows_product(gp, ncols, out_up)
+    for k in range(1, n_t):
+        arrived(grecv.at[k - 1], gt_s.at[k - 1], gt_r.at[k - 1])
+    total = gsum[...] + grecv[0] + grecv[1] + grecv[2]
+    total = jnp.sum(total, axis=0, keepdims=True) / gain_own[...].astype(jnp.float32)
+    gshare[d] = jnp.broadcast_to(total, (8, columns))
+    for k in order:
+        send(gshare.at[d], gshare.at[d], gd_s.at[k], gd_r.at[k], dp_peer(k))
+    share_wait(1, hid)
+    rows_product(hid, gcols, out_down)
+
+    for k in order:
+        arrived(gnrows.at[:, cols_of(lax.rem(d - k + n_dp, n_dp))], back_s.at[k], back_r.at[k])
+    inv = inv_rms[...]
+    dots = jnp.zeros((rows, 1), jnp.float32)
+    for i in range(n_dp):
+        s = pl.ds(i * columns, columns)
+        dots = dots + jnp.sum(
+            gnrows[:, s].astype(jnp.float32) * gain_row[:, s].astype(jnp.float32)
+            * (tokens[:, s].astype(jnp.float32) * inv), axis=-1, keepdims=True)
+    mean_term = dots / tokens.shape[1]
+    for i in range(n_dp):
+        s = pl.ds(i * columns, columns)
+        unit = tokens[:, s].astype(jnp.float32) * inv
+        grad_unit = gnrows[:, s].astype(jnp.float32) * gain_row[:, s].astype(jnp.float32)
+        out_tokens[:, s] = (inv * (grad_unit - unit * mean_term)).astype(jnp.bfloat16)
+    for k in order:
+        arrived(gshare.at[lax.rem(d - k + n_dp, n_dp)], gd_s.at[k], gd_r.at[k])
+    for i in range(n_dp):
+        out_gain[pl.ds(i, 1), :] = gshare[i, 0:1, :]
+    for copy in sent:
+        copy.wait_send()
+
+
+def fused(tokens, gain, up_weight, down_weight, grad_out):
+    rows, width = tokens.shape
+    hidden, columns = up_weight.shape
+    n_dp, n_t = width // columns, 4
+    block, chunk = n_dp * rows, n_t * rows
+    count = n_t * block
+    gain_row = gain.reshape(1, width)
+    gain_own = lax.dynamic_slice_in_dim(gain_row, lax.axis_index("dp") * columns, columns, 1)
+    vmem = pl.BlockSpec(memory_space=pltpu.VMEM)
+    bf16, f32 = jnp.bfloat16, jnp.float32
+    pairs = [(2, 8), (2, 3), (2, 4), (2, 3), (2, 4), (2, 4), (3,), (8,), (3,), (8,)]
+    sems = []
+    for shape in pairs:
+        sems += [pltpu.SemaphoreType.DMA(shape), pltpu.SemaphoreType.DMA(shape)]
+    flops = 10 * count * hidden * columns
+    grad_tokens, grad_gain, grad_up, grad_down = pl.pallas_call(
+        kernel,
+        out_shape=(
+            jax.ShapeDtypeStruct((rows, width), bf16),
+            jax.ShapeDtypeStruct((n_dp, columns), f32),
+            jax.ShapeDtypeStruct((hidden, columns), bf16),
+            jax.ShapeDtypeStruct((hidden, columns), bf16),
+        ),
+        in_specs=[vmem] * 6,
+        out_specs=(vmem,) * 4,
+        scratch_shapes=[
+            pltpu.VMEM((rows, 1), f32),
+            pltpu.VMEM((rows, width), bf16),
+            pltpu.VMEM((count, columns), bf16),
+            pltpu.VMEM((count, columns), bf16),
+            pltpu.VMEM((2, 4, 2, hidden, chunk), bf16),
+            pltpu.VMEM((2, 4, hidden, chunk), bf16),
+            pltpu.VMEM((2, 3, hidden, chunk), bf16),
+            pltpu.VMEM((2, 3, hidden, chunk), bf16),
+            pltpu.VMEM((hidden, count), bf16),
+            pltpu.VMEM((hidden, count), bf16),
+            pltpu.VMEM((2, block, columns), bf16),
+            pltpu.VMEM((2, block, columns), bf16),
+            pltpu.VMEM((block, columns), bf16),
+            pltpu.VMEM((block, columns), bf16),
+            pltpu.VMEM((block, columns), f32),
+            pltpu.VMEM((block, columns), bf16),
+            pltpu.VMEM((rows, width), bf16),
+            pltpu.VMEM((8, columns), f32),
+            pltpu.VMEM((3, 8, columns), f32),
+            pltpu.VMEM((n_dp, 8, columns), f32),
+            *sems,
+        ],
+        compiler_params=pltpu.CompilerParams(
+            collective_id=0, has_side_effects=True, vmem_limit_bytes=56 * 1024 * 1024
+        ),
+        cost_estimate=pl.CostEstimate(flops=flops, bytes_accessed=8 * hidden * columns, transcendentals=0),
+    )(tokens, gain_row, gain_own, up_weight, down_weight, grad_out)
+    return (grad_tokens, grad_gain.reshape(width), grad_up, grad_down)
+
+
 def solution(mesh):
+    n_dp, n_tensor = mesh.shape["dp"], mesh.shape["tensor"]
+
+    def step(tokens, gain, up_weight, down_weight, grad_out):
+        hidden, columns = up_weight.shape
+        fits = columns % 128 == 0 and hidden % 16 == 0 and tokens.shape[0] % 16 == 0
+        if fits and n_tensor == 4 and n_dp == 8:
+            return fused(tokens, gain, up_weight, down_weight, grad_out)
+        return local(tokens, gain, up_weight, down_weight, grad_out)
+
     rows = P(("dp", "tensor"), None)
     weights = P("tensor", "dp")
     return jax.shard_map(
-        local,
+        step,
         mesh=mesh,
         in_specs=(rows, P(), weights, weights, rows),
         out_specs=(rows, P(), weights, weights),

time: 398 us -> 164 us (0.41)
  waiting for transfers between devices: 264 us -> 0 us
  Pallas kernels: 0 us -> 154 us
  blocking collectives: 82.7 us -> 0 us
  matrix products: 21.6 us -> 0 us
  between operations: 14.2 us -> 0.65 us
  starting transfers between devices: 5.78 us -> 0 us
    pallas_call x0 -> x1, Pallas kernels: none -> 154 us  [fused(): pl.pallas_call(kernel, out_shape=(jax.ShapeDtypeStruct((rows, width), bf1...]
    unnamed x9 -> x0, waiting for transfers between devices: 130 us -> none
    all_gather x4 -> x0, waiting for transfers between devices: 102 us -> none  [the longest x1 40.5 us: local(): grad_pre = lax.all_gather(grad_pre_part, 'dp', axis=0, tiled=True)]
    all_to_all x2 -> x0, blocking collectives: 43.1 us -> none  [to_columns(): part = lax.all_to_all(rows, 'dp', split_axis=1, concat_axis=0, tiled=True)]
    psum x1 -> x0, blocking collectives: 39.6 us -> none  [local(): lax.psum(jnp.sum(grad_normed * unit_rows, axis=0), ('dp', 'tensor'))]
    reduce_scatter x1 -> x0, waiting for transfers between devices: 31.3 us -> none  [local(): lax.psum_scatter(grad_normed_part, 'tensor', scatter_dimension=0, tiled=T...]
    dot_general x5 -> x0, matrix products: 21.6 us -> none  [the longest x1 4.9 us: local(): jnp.dot(grad_pre, up_weight, preferred_element_type=jnp.float32)]
    all_to_all x1 -> x0, starting transfers between devices: 5.49 us -> none  [local(): lax.all_to_all(grad_normed, 'dp', split_axis=0, concat_axis=1, tiled=True)]
  transfers between devices with their start and end apart: 8 -> 0, of which waited for: 7 -> 0; matrix products, arithmetic and copies ran while one was open for 5% -> 0% of each run, Pallas kernels for 0% -> 0%
where the time goes in v2:
time: 164 us
  Pallas kernels  154 us (94%)
  local copies, waits for them, and re-layouts  9.69 us (6%)
    pallas_call x1, Pallas kernels, fused(): pl.pallas_call(kernel, out_shape=(jax.ShapeDtypeStruct((rows, width), bf1...  154 us
    unnamed x5, local copies, waits for them, and re-layouts  5.57 us

profile of v2, /device:TPU:0, one launch (start us, length us, event | category | flops | bytes accessed | tf_op | source)
XLA Modules:
  0.0 164.0 jit_solution(14669249667591468308)
XLA Ops:
  0.6 0.8 dynamic-slice.3
  1.4 0.6 dynamic_slice.3.gain_own
  2.0 1.4 reshape.15.gain_row
  3.4 153.6 %shard_map.84 = (bf16[32,9216]{1,0:T(8,128)(2,1)}, f32[8,1152]{1,0:T(8,128)}, bf16[576,1152]{1,0:T(8,128)(2,1)}, bf16[576,1152]{1,0:T(8,128)(2,1)}) custom-call(bf16[32,9216]{1,0:T(8,128)(2,1)} %tokens.1, bf16[1,9216]{1,0:T(2,128)(2,1)} %reshape.15.gain_row, bf16[1,1152]{1,0:T(2,128)(2,1)} %dynamic_slice.3.gain_own, bf16[576,1152]{1,0:T(8,128)(2,1)} %up.1, ...), custom_call_target="tpu_custom_call" | custom-call | flops 6794772480 | bytes 5308416 | tf_op jit(solution)/shard_map/pallas_call | solution.py:334
  157.0 1.4 reshape.16
  158.4 1.9 %copy.12 = bf16[32,9216]{1,0:T(8,128)(2,1)} copy(bf16[32,9216]{1,0:T(8,128)(2,1)} %get-tuple-element.16) | data formatting | bytes 1179648
  160.3 0.0 copy-start
  160.3 2.6 %copy.13 = bf16[576,1152]{1,0:T(8,128)(2,1)} copy(bf16[576,1152]{1,0:T(8,128)(2,1)} %get-tuple-element.18) | data formatting | bytes 2654208
  162.9 0.0 copy-done
  162.9 1.1 copy.14
Async XLA Ops:
  160.3 2.6 %copy-start = (bf16[576,1152]{1,0:T(8,128)(2,1)S(1)}, bf16[576,1152]{1,0:T(8,128)(2,1)}, u32[]{:S(2)}) copy-start(bf16[576,1152]{1,0:T(8,128)(2,1)} %get-tuple-element.19) | copy-start | bytes 3981316

commit v3 on v2

--- a/solution.py
+++ b/solution.py
@@ -61,12 +61,12 @@
 
 
 def kernel(
-    tokens, gain_row, gain_own, up, down, grad_out,
+    tokens, gain, up, down, grad_out,
     out_tokens, out_gain, out_up, out_down,
-    inv_rms, normed, ncols, gcols, part, recvx, sumz, recvz, gp, hid,
+    inv_rms, gain_row, normed, ncols, gcols, part, recvx, sumz, recvz, gp, hid,
     esend, ecore, ysend, ey, gnf, gnb, gnrows, gsum, grecv, gshare,
     a2a_s, a2a_r, tens_s, tens_r, x_s, x_r, z_s, z_r, gz_s, gz_r, gx_s, gx_r,
-    e_s, e_r, back_s, back_r, gt_s, gt_r, gd_s, gd_r,
+    e_s, e_r, ey_s, ey_r, back_s, back_r, gt_s, gt_r, gd_s, gd_r,
 ):
     n_dp, n_t, n_z = 8, 4, 4
     rows, columns = tokens.shape[0], up.shape[1]
@@ -109,9 +109,6 @@
     def rows_of(i, size):
         return pl.ds(pl.multiple_of(i * size, 32), size)
 
-    def lanes_of(i):
-        return pl.ds(pl.multiple_of(i * chunk, 128), chunk)
-
     barrier = pltpu.get_barrier_semaphore()
     for k in range(1, n_dp):
         pl.semaphore_signal(barrier, inc=1, device_id=dp_peer(k), device_id_type=MESH)
@@ -125,37 +122,42 @@
         send(grad_out.at[:, cols_of(lax.rem(d + k, n_dp))], gcols.at[own_rows],
              a2a_s.at[0, k], a2a_r.at[0, k], dp_peer(k))
     gcols[own_rows, :] = grad_out[:, cols_of(d)]
+    gain_row[...] = gain[...].astype(jnp.float32).reshape(1, tokens.shape[1])
     floated = tokens[...].astype(jnp.float32)
     inv_rms[...] = lax.rsqrt(jnp.mean(floated * floated, axis=-1, keepdims=True) + epsilon)
     for i in range(n_dp):
         s = pl.ds(i * columns, columns)
         normed[:, s] = (
-            tokens[:, s].astype(jnp.float32) * inv_rms[...] * gain_row[:, s].astype(jnp.float32)
+            tokens[:, s].astype(jnp.float32) * inv_rms[...] * gain_row[:, s]
         ).astype(jnp.bfloat16)
-    for k in order:
+    for k in order[:3]:
         send(normed.at[:, cols_of(lax.rem(d + k, n_dp))], ncols.at[own_rows],
              a2a_s.at[1, k], a2a_r.at[1, k], dp_peer(k))
     ncols[own_rows, :] = normed[:, cols_of(d)]
 
-    own_block = rows_of(t, block)
-    y_block = rows_of((1 - y) * 2 + c, block)
-    core_block = rows_of(y * 2 + 1 - c, block)
-    far_block = rows_of((1 - y) * 2 + 1 - c, block)
-
-    def spread(a, buf):
-        for k in order:
-            arrived(buf.at[rows_of(t * n_dp + lax.rem(d - k + n_dp, n_dp), rows)],
-                    a2a_s.at[a, k], a2a_r.at[a, k])
-        send(buf.at[own_block], buf.at[own_block], tens_s.at[a, 0], tens_r.at[a, 0], y_peer)
-        send(buf.at[own_block], buf.at[own_block], tens_s.at[a, 1], tens_r.at[a, 1], core_peer)
+    core_t, y_t, far_t = y * 2 + 1 - c, (1 - y) * 2 + c, (1 - y) * 2 + 1 - c
+
+    def piece(owner, k):
+        return rows_of(owner * n_dp + lax.rem(d - k + n_dp, n_dp), rows)
+
+    def spread(a, buf, ks):
+        for k in ks:
+            p = piece(t, k)
+            if k:
+                arrived(buf.at[p], a2a_s.at[a, k], a2a_r.at[a, k])
+            send(buf.at[p], buf.at[p], tens_s.at[a, 0, k], tens_r.at[a, 0, k], y_peer)
+            send(buf.at[p], buf.at[p], tens_s.at[a, 1, k], tens_r.at[a, 1, k], core_peer)
 
     def spread_far(a, buf):
-        arrived(buf.at[y_block], tens_s.at[a, 0], tens_r.at[a, 0])
-        send(buf.at[y_block], buf.at[y_block], tens_s.at[a, 2], tens_r.at[a, 2], core_peer)
-
-    def spread_wait(a, buf):
-        arrived(buf.at[core_block], tens_s.at[a, 1], tens_r.at[a, 1])
-        arrived(buf.at[far_block], tens_s.at[a, 2], tens_r.at[a, 2])
+        for k in (0,) + order:
+            p = piece(y_t, k)
+            arrived(buf.at[p], tens_s.at[a, 0, k], tens_r.at[a, 0, k])
+            send(buf.at[p], buf.at[p], tens_s.at[a, 2, k], tens_r.at[a, 2, k], core_peer)
+
+    def spread_wait(a, buf, which):
+        for k in (0,) + order:
+            p = piece(core_t if which == 1 else far_t, k)
+            arrived(buf.at[p], tens_s.at[a, which, k], tens_r.at[a, which, k])
 
     def product(a, buf, weight, i):
         prod = lax.dot_general(
@@ -165,13 +167,7 @@
         part[a, i, 0] = prod[:, :chunk]
         part[a, i, 1] = prod[:, chunk:]
 
-    def to_x(a, i):
         send(part.at[a, i, 1 - x], recvx.at[a, i], x_s.at[a, i], x_r.at[a, i], x_peer)
-
-    def products(a, buf, weight):
-        for i in range(n_z):
-            product(a, buf, weight, i)
-            to_x(a, i)
 
     def x_sum(a, i):
         return part[a, i, x].astype(jnp.float32) + recvx[a, i].astype(jnp.float32)
@@ -195,73 +191,99 @@
             total = total + recvz[a, k, s, :].astype(jnp.float32)
         return total
 
-    spread(0, gcols)
+    spread(0, gcols, (0,) + order)
+    for k in order[3:]:
+        send(normed.at[:, cols_of(lax.rem(d + k, n_dp))], ncols.at[own_rows],
+             a2a_s.at[1, k], a2a_r.at[1, k], dp_peer(k))
+    product(0, gcols, down, t)
+    spread_wait(0, gcols, 1)
+    product(0, gcols, down, core_t)
+    spread(1, ncols, (0,))
     spread_far(0, gcols)
-    spread_wait(0, gcols)
-    products(0, gcols, down)
-    spread(1, ncols)
+    product(0, gcols, down, y_t)
+    spread(1, ncols, order[:3])
+    spread_wait(0, gcols, 2)
+    product(0, gcols, down, far_t)
+    spread(1, ncols, order[3:])
+    product(1, ncols, up, t)
     to_z(0)
     spread_far(1, ncols)
-    spread_wait(1, ncols)
-    products(1, ncols, up)
+    spread_wait(1, ncols, 1)
+    product(1, ncols, up, core_t)
+    product(1, ncols, up, y_t)
+    spread_wait(1, ncols, 2)
+    product(1, ncols, up, far_t)
     to_z(1)
     z_wait(0)
     z_wait(1)
 
-    own_lanes = lanes_of(d)
     whole = pl.ds(0, hidden)
     lifted = jnp.maximum(z_sum(1, whole), 0.0)
-    gp[:, own_lanes] = (z_sum(0, whole) * (2.0 * lifted)).astype(jnp.bfloat16)
-    hid[:, own_lanes] = (lifted * lifted).astype(jnp.bfloat16)
+    gp[d] = (z_sum(0, whole) * (2.0 * lifted)).astype(jnp.bfloat16)
+    hid[d] = (lifted * lifted).astype(jnp.bfloat16)
 
     def share(a, buf):
         for k in (2, 1, 3):
-            send(buf.at[:, own_lanes], buf.at[:, own_lanes], gz_s.at[a, k], gz_r.at[a, k],
+            send(buf.at[d], buf.at[d], gz_s.at[a, k], gz_r.at[a, k],
                  z_peer(k))
-        send(buf.at[:, own_lanes], buf.at[:, own_lanes], gx_s.at[a, 0], gx_r.at[a, 0], x_peer)
+        send(buf.at[d], buf.at[d], gx_s.at[a, 0], gx_r.at[a, 0], x_peer)
 
     def z_lanes(k, side):
-        return lanes_of(lax.rem(z - k + n_z, n_z) * 2 + side)
+        return lax.rem(z - k + n_z, n_z) * 2 + side
 
     def share_far(a, buf):
         for k in (1, 3, 2):
             s = z_lanes(k, x)
-            arrived(buf.at[:, s], gz_s.at[a, k], gz_r.at[a, k])
-            send(buf.at[:, s], buf.at[:, s], gx_s.at[a, k], gx_r.at[a, k], x_peer)
-
-    def share_wait(a, buf):
-        for k in range(n_z):
-            arrived(buf.at[:, z_lanes(k, 1 - x)], gx_s.at[a, k], gx_r.at[a, k])
+            arrived(buf.at[s], gz_s.at[a, k], gz_r.at[a, k])
+            send(buf.at[s], buf.at[s], gx_s.at[a, k], gx_r.at[a, k], x_peer)
+
+    def share_wait(a, buf, i):
+        k = lax.rem(z - i + n_z, n_z)
+        arrived(buf.at[i * 2 + 1 - x], gx_s.at[a, k], gx_r.at[a, k])
 
     share(0, gp)
+    share_far(0, gp)
     share(1, hid)
-    share_far(0, gp)
-    share_wait(0, gp)
 
     def input_part(i):
         return lax.dot_general(
-            gp[:, pl.ds(pl.multiple_of(i * block, 128), block)], up[...],
+            jnp.concatenate([gp[i * 2], gp[i * 2 + 1]], axis=1), up[...],
             (((0,), (0,)), ((), ())), preferred_element_type=jnp.float32,
         )
 
     for h in range(2):
-        q = 1 - y if h == 0 else y
-        esend[h] = input_part(q * 2 + 1 - c).astype(jnp.bfloat16)
+        i = far_t if h == 0 else core_t
+        share_wait(0, gp, i)
+        esend[h] = input_part(i).astype(jnp.bfloat16)
         send(esend.at[h], ecore.at[h], e_s.at[h], e_r.at[h], core_peer)
-    gnf[...] = input_part((1 - y) * 2 + c)
+    share_wait(0, gp, y_t)
+    gnf[...] = input_part(y_t)
     arrived(ecore.at[0], e_s.at[0], e_r.at[0])
-    ysend[...] = (gnf[...] + ecore[0].astype(jnp.float32)).astype(jnp.bfloat16)
-    send(ysend, ey, e_s.at[2], e_r.at[2], y_peer)
+
+    def part_rows(k):
+        return rows_of(lax.rem(z + k, n_z), 2 * rows)
+
+    parts = (2, 3, 1, 0)
+    for k in parts:
+        r = part_rows(k)
+        ysend[r, :] = (gnf[r, :] + ecore[0, r, :].astype(jnp.float32)).astype(jnp.bfloat16)
+        send(ysend.at[r], ey.at[r], ey_s.at[k], ey_r.at[k], y_peer)
+    share_wait(0, gp, t)
     gnf[...] = input_part(t)
     arrived(ecore.at[1], e_s.at[1], e_r.at[1])
-    gnf[...] = gnf[...] + ecore[1].astype(jnp.float32)
+    for k in parts:
+        r = part_rows(k)
+        arrived(ey.at[r], ey_s.at[k], ey_r.at[k])
+        total = gnf[r, :] + ecore[1, r, :].astype(jnp.float32) + ey[r, :].astype(jnp.float32)
+        gnf[r, :] = total
+        gnb[r, :] = total.astype(jnp.bfloat16)
+        i = lax.rem(z + k, n_z) * 2
+        send(gnb.at[rows_of(i + 1 - x, rows)], gnrows.at[:, cols_of(d)],
+             back_s.at[k, 0], back_r.at[k, 0], (i + 1 - x, t))
+        if k:
+            send(gnb.at[rows_of(i + x, rows)], gnrows.at[:, cols_of(d)],
+                 back_s.at[k, 1], back_r.at[k, 1], (i + x, t))
     share_far(1, hid)
-    arrived(ey, e_s.at[2], e_r.at[2])
-    gnf[...] = gnf[...] + ey[...].astype(jnp.float32)
-    gnb[...] = gnf[...].astype(jnp.bfloat16)
-    for k in order:
-        send(gnb.at[rows_of(lax.rem(d + k, n_dp), rows)], gnrows.at[:, cols_of(d)],
-             back_s.at[k], back_r.at[k], dp_peer(k))
     gnrows[:, cols_of(d)] = gnb[rows_of(d, rows), :]
 
     total = jnp.zeros((8, columns), jnp.float32)
@@ -276,42 +298,47 @@
 
     def rows_product(left, right, out):
         half = columns // 3
+        lanes = jnp.concatenate([left[i] for i in range(n_dp)], axis=1)
         for i in range(3):
             s = pl.ds(i * half, half)
             out[:, s] = jnp.dot(
-                left[...], right[:, s], preferred_element_type=jnp.float32
+                lanes, right[:, s], preferred_element_type=jnp.float32
             ).astype(jnp.bfloat16)
 
     rows_product(gp, ncols, out_up)
     for k in range(1, n_t):
         arrived(grecv.at[k - 1], gt_s.at[k - 1], gt_r.at[k - 1])
     total = gsum[...] + grecv[0] + grecv[1] + grecv[2]
-    total = jnp.sum(total, axis=0, keepdims=True) / gain_own[...].astype(jnp.float32)
+    total = jnp.sum(total, axis=0, keepdims=True) / gain_row[:, cols_of(d)]
     gshare[d] = jnp.broadcast_to(total, (8, columns))
     for k in order:
         send(gshare.at[d], gshare.at[d], gd_s.at[k], gd_r.at[k], dp_peer(k))
-    share_wait(1, hid)
+    for i in range(n_z):
+        share_wait(1, hid, i)
     rows_product(hid, gcols, out_down)
 
-    for k in order:
-        arrived(gnrows.at[:, cols_of(lax.rem(d - k + n_dp, n_dp))], back_s.at[k], back_r.at[k])
+    for k in parts:
+        i = lax.rem(z - k + n_z, n_z) * 2
+        arrived(gnrows.at[:, cols_of(i + 1 - x)], back_s.at[k, 0], back_r.at[k, 0])
+        if k:
+            arrived(gnrows.at[:, cols_of(i + x)], back_s.at[k, 1], back_r.at[k, 1])
     inv = inv_rms[...]
     dots = jnp.zeros((rows, 1), jnp.float32)
     for i in range(n_dp):
         s = pl.ds(i * columns, columns)
         dots = dots + jnp.sum(
-            gnrows[:, s].astype(jnp.float32) * gain_row[:, s].astype(jnp.float32)
+            gnrows[:, s].astype(jnp.float32) * gain_row[:, s]
             * (tokens[:, s].astype(jnp.float32) * inv), axis=-1, keepdims=True)
     mean_term = dots / tokens.shape[1]
     for i in range(n_dp):
         s = pl.ds(i * columns, columns)
         unit = tokens[:, s].astype(jnp.float32) * inv
-        grad_unit = gnrows[:, s].astype(jnp.float32) * gain_row[:, s].astype(jnp.float32)
+        grad_unit = gnrows[:, s].astype(jnp.float32) * gain_row[:, s]
         out_tokens[:, s] = (inv * (grad_unit - unit * mean_term)).astype(jnp.bfloat16)
     for k in order:
         arrived(gshare.at[lax.rem(d - k + n_dp, n_dp)], gd_s.at[k], gd_r.at[k])
     for i in range(n_dp):
-        out_gain[pl.ds(i, 1), :] = gshare[i, 0:1, :]
+        out_gain[pl.ds(i * columns, columns)] = gshare[i, 0:1, :].reshape(columns)
     for copy in sent:
         copy.wait_send()
 
@@ -322,11 +349,9 @@
     n_dp, n_t = width // columns, 4
     block, chunk = n_dp * rows, n_t * rows
     count = n_t * block
-    gain_row = gain.reshape(1, width)
-    gain_own = lax.dynamic_slice_in_dim(gain_row, lax.axis_index("dp") * columns, columns, 1)
     vmem = pl.BlockSpec(memory_space=pltpu.VMEM)
     bf16, f32 = jnp.bfloat16, jnp.float32
-    pairs = [(2, 8), (2, 3), (2, 4), (2, 3), (2, 4), (2, 4), (3,), (8,), (3,), (8,)]
+    pairs = [(2, 8), (2, 3, 8), (2, 4), (2, 3), (2, 4), (2, 4), (2,), (4,), (4, 2), (3,), (8,)]
     sems = []
     for shape in pairs:
         sems += [pltpu.SemaphoreType.DMA(shape), pltpu.SemaphoreType.DMA(shape)]
@@ -335,14 +360,15 @@
         kernel,
         out_shape=(
             jax.ShapeDtypeStruct((rows, width), bf16),
-            jax.ShapeDtypeStruct((n_dp, columns), f32),
+            jax.ShapeDtypeStruct((width,), f32),
             jax.ShapeDtypeStruct((hidden, columns), bf16),
             jax.ShapeDtypeStruct((hidden, columns), bf16),
         ),
-        in_specs=[vmem] * 6,
+        in_specs=[vmem] * 5,
         out_specs=(vmem,) * 4,
         scratch_shapes=[
             pltpu.VMEM((rows, 1), f32),
+            pltpu.VMEM((1, width), f32),
             pltpu.VMEM((rows, width), bf16),
             pltpu.VMEM((count, columns), bf16),
             pltpu.VMEM((count, columns), bf16),
@@ -350,8 +376,8 @@
             pltpu.VMEM((2, 4, hidden, chunk), bf16),
             pltpu.VMEM((2, 3, hidden, chunk), bf16),
             pltpu.VMEM((2, 3, hidden, chunk), bf16),
-            pltpu.VMEM((hidden, count), bf16),
-            pltpu.VMEM((hidden, count), bf16),
+            pltpu.VMEM((n_dp, hidden, chunk), bf16),
+            pltpu.VMEM((n_dp, hidden, chunk), bf16),
             pltpu.VMEM((2, block, columns), bf16),
             pltpu.VMEM((2, block, columns), bf16),
             pltpu.VMEM((block, columns), bf16),
@@ -368,8 +394,8 @@
             collective_id=0, has_side_effects=True, vmem_limit_bytes=56 * 1024 * 1024
         ),
         cost_estimate=pl.CostEstimate(flops=flops, bytes_accessed=8 * hidden * columns, transcendentals=0),
-    )(tokens, gain_row, gain_own, up_weight, down_weight, grad_out)
-    return (grad_tokens, grad_gain.reshape(width), grad_up, grad_down)
+    )(tokens, gain, up_weight, down_weight, grad_out)
+    return (grad_tokens, grad_gain, grad_up, grad_down)
 
 
 def solution(mesh):

time: 164 us -> 143 us (0.87)
  the two profiles are of different devices: /device:TPU:0 before, /device:TPU:18 now
where the time goes in v3:
time: 143 us
  Pallas kernels  135 us (94%)
  local copies, waits for them, and re-layouts  6.96 us (5%)
    pallas_call x1, Pallas kernels, fused(): pl.pallas_call(kernel, out_shape=(jax.ShapeDtypeStruct((rows, width), bf1...  135 us
    unnamed x6, local copies, waits for them, and re-layouts  6.96 us

profile of v3, /device:TPU:18, one launch (start us, length us, event | category | flops | bytes accessed | tf_op | source)
XLA Modules:
  0.0 142.6 jit_solution(7695002640290097428)
XLA Ops:
  0.6 135.0 %shard_map.84 = (bf16[32,9216]{1,0:T(8,128)(2,1)}, f32[9216]{0:T(1024)}, bf16[576,1152]{1,0:T(8,128)(2,1)}, bf16[576,1152]{1,0:T(8,128)(2,1)}) custom-call(bf16[32,9216]{1,0:T(8,128)(2,1)} %tokens.1, bf16[9216]{0:T(1024)(128)(2,1)} %gain.1, bf16[576,1152]{1,0:T(8,128)(2,1)} %up.1, bf16[576,1152]{1,0:T(8,128)(2,1)} %down.1, bf16[32,9216]{1,0:T(8,128)(2,1)} %grad_out.1), custom_call_target="tpu_custom_call" | custom-call | flops 6794772480 | bytes 5308416 | tf_op jit(solution)/shard_map/pallas_call | solution.py:359
  135.6 1.9 %copy.13 = bf16[32,9216]{1,0:T(8,128)(2,1)} copy(bf16[32,9216]{1,0:T(8,128)(2,1)} %get-tuple-element.8) | data formatting | bytes 1179648
  137.5 1.4 copy.14
  138.9 0.0 copy-start
  138.9 2.6 %copy.15 = bf16[576,1152]{1,0:T(8,128)(2,1)} copy(bf16[576,1152]{1,0:T(8,128)(2,1)} %get-tuple-element.10) | data formatting | bytes 2654208
  141.5 0.0 copy-done
  141.5 1.1 copy.16
Async XLA Ops:
  138.9 2.6 %copy-start = (bf16[576,1152]{1,0:T(8,128)(2,1)S(1)}, bf16[576,1152]{1,0:T(8,128)(2,1)}, u32[]{:S(2)}) copy-start(bf16[576,1152]{1,0:T(8,128)(2,1)} %get-tuple-element.11) | copy-start | bytes 3981316

commit v4 on v3

--- a/solution.py
+++ b/solution.py
@@ -172,13 +172,20 @@
     def x_sum(a, i):
         return part[a, i, x].astype(jnp.float32) + recvx[a, i].astype(jnp.float32)
 
-    def to_z(a):
-        for k in (2, 3, 1):
-            i = lax.rem(z + k, n_z)
+    def to_z(a, i):
+        k = lax.rem(i - z + n_z, n_z)
+
+        @pl.when(k != 0)
+        def _():
             arrived(recvx.at[a, i], x_s.at[a, i], x_r.at[a, i])
             sumz[a, k - 1] = x_sum(a, i).astype(jnp.bfloat16)
-            send(sumz.at[a, k - 1], recvz.at[a, k - 1], z_s.at[a, k - 1], z_r.at[a, k - 1],
-                 z_peer(k))
+            z_copy(a, k).start()
+
+    def z_copy(a, k):
+        return pltpu.make_async_remote_copy(
+            src_ref=sumz.at[a, k - 1], dst_ref=recvz.at[a, k - 1], send_sem=z_s.at[a, k - 1],
+            recv_sem=z_r.at[a, k - 1], device_id=z_peer(k), device_id_type=MESH,
+        )
 
     def z_wait(a):
         arrived(recvx.at[a, z], x_s.at[a, z], x_r.at[a, z])
@@ -206,14 +213,18 @@
     product(0, gcols, down, far_t)
     spread(1, ncols, order[3:])
     product(1, ncols, up, t)
-    to_z(0)
-    spread_far(1, ncols)
+    for i in (t, core_t, y_t, far_t):
+        to_z(0, i)
     spread_wait(1, ncols, 1)
     product(1, ncols, up, core_t)
+    to_z(1, t)
+    to_z(1, core_t)
+    spread_far(1, ncols)
     product(1, ncols, up, y_t)
     spread_wait(1, ncols, 2)
     product(1, ncols, up, far_t)
-    to_z(1)
+    to_z(1, y_t)
+    to_z(1, far_t)
     z_wait(0)
     z_wait(1)
 
@@ -268,6 +279,7 @@
         r = part_rows(k)
         ysend[r, :] = (gnf[r, :] + ecore[0, r, :].astype(jnp.float32)).astype(jnp.bfloat16)
         send(ysend.at[r], ey.at[r], ey_s.at[k], ey_r.at[k], y_peer)
+    share_far(1, hid)
     share_wait(0, gp, t)
     gnf[...] = input_part(t)
     arrived(ecore.at[1], e_s.at[1], e_r.at[1])
@@ -283,7 +295,6 @@
         if k:
             send(gnb.at[rows_of(i + x, rows)], gnrows.at[:, cols_of(d)],
                  back_s.at[k, 1], back_r.at[k, 1], (i + x, t))
-    share_far(1, hid)
     gnrows[:, cols_of(d)] = gnb[rows_of(d, rows), :]
 
     total = jnp.zeros((8, columns), jnp.float32)
@@ -339,6 +350,9 @@
         arrived(gshare.at[lax.rem(d - k + n_dp, n_dp)], gd_s.at[k], gd_r.at[k])
     for i in range(n_dp):
         out_gain[pl.ds(i * columns, columns)] = gshare[i, 0:1, :].reshape(columns)
+    for a in range(2):
+        for k in (1, 2, 3):
+            z_copy(a, k).wait_send()
     for copy in sent:
         copy.wait_send()
 

time: 143 us -> 132 us (0.923)
  the two profiles are of different devices: /device:TPU:18 before, /device:TPU:0 now
where the time goes in v4:
time: 132 us
  Pallas kernels  124 us (94%)
  local copies, waits for them, and re-layouts  6.96 us (5%)
    pallas_call x1, Pallas kernels, fused(): pl.pallas_call(kernel, out_shape=(jax.ShapeDtypeStruct((rows, width), bf1...  124 us
    unnamed x6, local copies, waits for them, and re-layouts  6.96 us

profile of v4, /device:TPU:0, one launch (start us, length us, event | category | flops | bytes accessed | tf_op | source)
XLA Modules:
  0.0 132.1 jit_solution(556863294799570264)
XLA Ops:
  0.6 124.5 %shard_map.84 = (bf16[32,9216]{1,0:T(8,128)(2,1)}, f32[9216]{0:T(1024)}, bf16[576,1152]{1,0:T(8,128)(2,1)}, bf16[576,1152]{1,0:T(8,128)(2,1)}) custom-call(bf16[32,9216]{1,0:T(8,128)(2,1)} %tokens.1, bf16[9216]{0:T(1024)(128)(2,1)} %gain.1, bf16[576,1152]{1,0:T(8,128)(2,1)} %up.1, bf16[576,1152]{1,0:T(8,128)(2,1)} %down.1, bf16[32,9216]{1,0:T(8,128)(2,1)} %grad_out.1), custom_call_target="tpu_custom_call" | custom-call | flops 6794772480 | bytes 5308416 | tf_op jit(solution)/shard_map/pallas_call | solution.py:373
  125.1 1.9 %copy.13 = bf16[32,9216]{1,0:T(8,128)(2,1)} copy(bf16[32,9216]{1,0:T(8,128)(2,1)} %get-tuple-element.8) | data formatting | bytes 1179648
  127.0 1.4 %copy.14 = f32[9216]{0:T(1024)} copy(f32[9216]{0:T(1024)} %get-tuple-element.9) | data formatting | bytes 73728
  128.4 0.0 copy-start
  128.4 2.6 %copy.15 = bf16[576,1152]{1,0:T(8,128)(2,1)} copy(bf16[576,1152]{1,0:T(8,128)(2,1)} %get-tuple-element.10) | data formatting | bytes 2654208
  131.0 0.0 copy-done
  131.0 1.1 copy.16
Async XLA Ops:
  128.4 2.6 %copy-start = (bf16[576,1152]{1,0:T(8,128)(2,1)S(1)}, bf16[576,1152]{1,0:T(8,128)(2,1)}, u32[]{:S(2)}) copy-start(bf16[576,1152]{1,0:T(8,128)(2,1)} %get-tuple-element.11) | copy-start | bytes 3981316
